TPU v7x, 32 devices: a whole 2x2x4 slice. The times are simulated.
32 devices in a mesh: seq: 8 (over y, x, core), head: 4 (over z).
Axes of the slice: x: 2, y: 2, z: 4, core: 2. Of those that a mesh axis runs over, the one named last changes fastest.
Arguments:
- queries: bfloat16 [16384, 512], P('seq', 'head'), may hold values from -4 to 4
- key_rows: bfloat16 [16384, 512], P('seq', 'head'), may hold values from -4 to 4
- value_rows: bfloat16 [16384, 512], P('seq', 'head'), may hold values from -6 to 6
- norm_gain: float32 [512], P('head'), may hold values from 0.1 to 1.9
- out_grad: bfloat16 [16384, 512], P('seq', 'head'), may hold values from -6 to 6
Outputs:
- normed: bfloat16 [16384, 512], P('seq', 'head')
- query_grad: bfloat16 [16384, 512], P('seq', 'head')
- key_grad: bfloat16 [16384, 512], P('seq', 'head')
- value_grad: bfloat16 [16384, 512], P('seq', 'head')
All inputs are finite; a program needn't handle non-finite values.
Results may differ from a plain program's by a relative error of at most 0.0059.
Values sent between devices are 32-bit elements; how exact they have to be, the bound alone decides.
A program may use at most 64 MiB of HBM per device.

v0:
```python
import jax
import jax.numpy as jnp
from jax import lax
from jax.sharding import PartitionSpec as P

HEAD_DIM = 128
BLOCK = 512


def causal_mask(size):
    row_index = lax.broadcasted_iota(jnp.int32, (size, size), 0)
    col_index = lax.broadcasted_iota(jnp.int32, (size, size), 1)
    return row_index >= col_index


def body(queries, key_rows, value_rows, norm_gain, out_grad):
    tokens_here = queries.shape[0]
    heads_here = queries.shape[1] // HEAD_DIM
    blocks = tokens_here // BLOCK
    block_shape = (blocks, BLOCK, heads_here, HEAD_DIM)
    query4 = queries.reshape(block_shape)
    key4 = key_rows.reshape(block_shape)
    value4 = value_rows.reshape(block_shape)
    width_all = heads_here * HEAD_DIM * lax.axis_size("head")
    mask4 = causal_mask(BLOCK)[None, None]
    position = lax.axis_index("seq")
    states = jnp.einsum("bshd,bshe->bhde", key4, value4, preferred_element_type=jnp.float32)
    totals = jnp.sum(states, 0)
    piece = lax.all_gather(totals[None], "seq", axis=0, tiled=True)
    anchor = jnp.arange(piece.shape[0], dtype=jnp.int32)
    keep = (anchor < position)[:, None, None, None]
    earlier = jnp.sum(jnp.where(keep, piece, 0.0), 0)
    running = jnp.cumsum(states, 0)
    within = jnp.concatenate([jnp.zeros_like(states[:1]), running[:-1]], 0)
    prefix16 = (earlier[None] + within).astype(jnp.bfloat16)
    scores = jnp.einsum("bthd,bshd->bhts", query4, key4, preferred_element_type=jnp.float32)
    attn = jnp.where(mask4, scores, 0.0).astype(jnp.bfloat16)
    output = jnp.einsum("bhts,bshe->bthe", attn, value4, preferred_element_type=jnp.float32)
    output = output + jnp.einsum(
        "bthd,bhde->bthe", query4, prefix16, preferred_element_type=jnp.float32
    )
    gain4 = norm_gain.reshape(heads_here, HEAD_DIM)
    scaled = out_grad.reshape(block_shape).astype(jnp.float32) * gain4
    squares, products = lax.psum(
        (jnp.sum(output * output, (2, 3)), jnp.sum(scaled * output, (2, 3))), "head"
    )
    rstd = lax.rsqrt(squares / width_all + 1e-05)[:, :, None, None]
    normed = (output * rstd * gain4).astype(jnp.bfloat16).reshape(tokens_here, -1)
    mean_prod = (products / width_all)[:, :, None, None]
    dout = (rstd * scaled - output * rstd**3 * mean_prod).astype(jnp.bfloat16)
    grad_states = jnp.einsum("bthd,bthe->bhde", query4, dout, preferred_element_type=jnp.float32)
    grad_total = jnp.sum(grad_states, 0)
    piece = lax.all_gather(grad_total[None], "seq", axis=0, tiled=True)
    anchor = jnp.arange(piece.shape[0], dtype=jnp.int32)
    keep = (anchor > position)[:, None, None, None]
    later = jnp.sum(jnp.where(keep, piece, 0.0), 0)
    behind = jnp.cumsum(grad_states[::-1], 0)[::-1]
    after = jnp.concatenate([behind[1:], jnp.zeros_like(grad_states[:1])], 0)
    suffix16 = (later[None] + after).astype(jnp.bfloat16)
    bmat = jnp.einsum("bthe,bshe->bhts", dout, value4, preferred_element_type=jnp.float32)
    bmat = jnp.where(mask4, bmat, 0.0).astype(jnp.bfloat16)
    query_grad = jnp.einsum("bhts,bshd->bthd", bmat, key4, preferred_element_type=jnp.float32)
    query_grad = query_grad + jnp.einsum(
        "bthe,bhde->bthd", dout, prefix16, preferred_element_type=jnp.float32
    )
    key_grad = jnp.einsum("bhts,bthd->bshd", bmat, query4, preferred_element_type=jnp.float32)
    key_grad = key_grad + jnp.einsum(
        "bshe,bhde->bshd", value4, suffix16, preferred_element_type=jnp.float32
    )
    value_grad = jnp.einsum("bhts,bthe->bshe", attn, dout, preferred_element_type=jnp.float32)
    value_grad = value_grad + jnp.einsum(
        "bshd,bhde->bshe", key4, suffix16, preferred_element_type=jnp.float32
    )
    return (
        normed,
        query_grad.astype(jnp.bfloat16).reshape(tokens_here, -1),
        key_grad.astype(jnp.bfloat16).reshape(tokens_here, -1),
        value_grad.astype(jnp.bfloat16).reshape(tokens_here, -1),
    )


def solution(mesh):
    return jax.shard_map(
        body,
        mesh=mesh,
        in_specs=(
            P("seq", "head"),
            P("seq", "head"),
            P("seq", "head"),
            P("head"),
            P("seq", "head"),
        ),
        out_specs=(P("seq", "head"), P("seq", "head"), P("seq", "head"), P("seq", "head")),
        check_vma=False,
    )
```

profile of v0, /device:TPU:0, one launch (start us, length us, event | category | flops | bytes accessed | tf_op | source)
XLA Modules:
  0.0 71.4 jit_solution(403312878023820120)
XLA Ops:
  0.6 0.0 copy-start
  0.7 1.0 %copy-done = bf16[2048,128]{1,0:T(8,128)(2,1)S(1)} copy-done((bf16[2048,128]{1,0:T(8,128)(2,1)S(1)}, bf16[2048,128]{1,0:T(8,128)(2,1)}, u32[]{:S(2)}) %copy-start) | copy-done | bytes 524312
  1.7 0.1 iota_compare_fusion
  1.8 0.0 copy-start.9
  1.8 1.9 %select_convert_fusion.1 = bf16[4,512,512]{2,1,0:T(8,128)(2,1)S(1)} fusion(bf16[4,512,128]{2,1,0:T(8,128)(2,1)S(1)} %bitcast.81, bf16[4,512,128]{2,1,0:T(8,128)(2,1)} %bitcast.89, pred[512,512]{1,0:T(8,128)(4,1)S(1)} %iota_compare_fusion), kind=kOutput, calls=%fused_computation.1 | convolution fusion | flops 270532608 | bytes 3407872 | tf_op jit(solution)/shard_map/bthd,bshd->bhts/dot_general | solution.py:36
  3.7 1.7 %convolution_bitcast_fusion.2 = f32[4,128,512]{1,2,0:T(8,128)} fusion(bf16[4,512,512]{2,1,0:T(8,128)(2,1)S(1)} %select_convert_fusion.1, bf16[4,512,128]{2,1,0:T(8,128)(2,1)S(1)} %bitcast.85), kind=kOutput, calls=%fused_computation.4 | convolution fusion | flops 268435456 | bytes 3670016 | tf_op jit(solution)/shard_map/bhts,bshe->bthe/dot_general | solution.py:38
  5.4 0.3 fusion.26
  5.7 12.4 %all-gather = f32[1024,128]{1,0:T(8,128)} all-gather(f32[128,128]{1,0:T(8,128)S(1)} %get-tuple-element.12), channel_id=2, replica_groups=mesh['seq'=8,'head'=4] {'seq'}, dimensions={0}, use_global_device_ids=true | all-gather | bytes 589824 | tf_op jit(solution)/shard_map/all_gather | solution.py:29
  18.1 1.3 %copy.39 = f32[8,1,128,128]{2,0,3,1:T(8,128)S(1)} copy(f32[8,1,128,128]{3,2,0,1:T(8,128)} %bitcast.93) | data formatting | bytes 1048576 | tf_op jit(solution)/shard_map/all_gather | solution.py:29
  19.4 0.2 select_reduce_fusion
  19.6 0.1 copy.40
  19.7 0.2 fusion.14
  19.9 2.8 %fusion.9 = (f32[4,512]{1,0:T(4,128)S(1)}, f32[4,512]{1,0:T(4,128)S(1)}, f32[4,512,1,128]{3,1,0,2:T(8,128)}) fusion(bf16[4,512,1,128]{3,1,0,2:T(8,128)(2,1)} %bitcast.95, f32[128]{0:T(128)S(1)} %copy-done.10, f32[4,128,512]{1,2,0:T(8,128)} %convolution_bitcast_fusion.2, bf16[4,512,128]{2,1,0:T(8,128)(2,1)S(1)} %bitcast.82, ...), kind=kOutput, calls=%fused_computation.20 | convolution fusion | flops 69070848 | bytes 3424768 | tf_op jit(solution)/shard_map/bthd,bhde->bthe/dot_general | solution.py:39
  22.7 19.0 %all-reduce.2 = (f32[4,512]{1,0:T(4,128)S(1)}, f32[4,512]{1,0:T(4,128)S(1)}) all-reduce(f32[4,512]{1,0:T(4,128)S(1)} %get-tuple-element.5, f32[4,512]{1,0:T(4,128)S(1)} %get-tuple-element.4), channel_id=1, replica_groups=mesh['seq'=8,'head'=4] {'head'}, use_global_device_ids=true, to_apply=%region_4.5 | all-reduce | flops 4096 | bytes 32768 | tf_op jit(solution)/shard_map/psum | solution.py:44
  41.7 2.8 %fusion.10 = (bf16[4,512,128]{2,1,0:T(8,128)(2,1)S(1)}, bf16[4,512,1,128]{3,1,0,2:T(8,128)(2,1)}) fusion(f32[4,512,1,128]{3,1,0,2:T(8,128)} %get-tuple-element.14, f32[4,512]{1,0:T(4,128)S(1)} %get-tuple-element.17, f32[4,512]{1,0:T(4,128)S(1)} %get-tuple-element.10, f32[128]{0:T(128)S(1)} %copy-done.10, f32[4,512]{1,0:T(4,128)S(1)} %get-tuple-element.11, ...), kind=kLoop, calls=%fused_computation.24 | loop fusion | flops 2621440 | bytes 2646528 | tf_op jit(solution)/shard_map/reshape.36
  44.5 1.5 %fusion.28 = f32[4,128,512]{2,1,0:T(8,128)} fusion(bf16[4,512,128]{2,1,0:T(8,128)(2,1)S(1)} %get-tuple-element.8, bf16[4,512,512]{2,1,0:T(8,128)(2,1)S(1)} %select_convert_fusion.1), kind=kOutput, calls=%fused_computation.47 | convolution fusion | flops 268435456 | bytes 3670016 | tf_op jit(solution)/shard_map/bhts,bthe->bshe/dot_general | solution.py:70
  46.0 1.0 %fusion.27 = (f32[128,128]{0,1:T(8,128)S(1)}, f32[4,128,128]{1,2,0:T(8,128)}) fusion(bf16[4,512,128]{2,1,0:T(8,128)(2,1)S(1)} %get-tuple-element.8, bf16[4,512,128]{2,1,0:T(8,128)(2,1)S(1)} %bitcast.84), kind=kOutput, calls=%fused_computation.46 | convolution fusion | flops 67158016 | bytes 1376256 | tf_op jit(solution)/shard_map/bthd,bthe->bhde/dot_general | solution.py:51
  47.1 11.0 %all-gather.1 = f32[1024,128]{0,1:T(8,128)S(1)} all-gather(f32[128,128]{0,1:T(8,128)S(1)} %get-tuple-element.15), channel_id=3, replica_groups=mesh['seq'=8,'head'=4] {'seq'}, dimensions={0}, use_global_device_ids=true | all-gather | bytes 589824 | tf_op jit(solution)/shard_map/all_gather | solution.py:53
  58.0 0.1 copy.59
  58.1 0.8 %fusion.11 = f32[128,128]{0,1:T(8,128)} fusion(f32[16,8,8,128]{3,2,1,0:T(8,128)S(1)} %copy.59, pred[8]{0:T(512)(128)(4,1)S(1)} %iota_compare_fusion.1), kind=kLoop, calls=%fused_computation.26 | loop fusion | flops 245760 | bytes 589832 | tf_op jit(solution)/shard_map/reduce_sum | solution.py:56
  59.0 1.0 %reverse.4 = f32[4,128,128]{1,2,0:T(8,128)S(1)} reverse(f32[4,128,128]{1,2,0:T(8,128)} %get-tuple-element.16), dimensions={0} | reverse | bytes 524288 | tf_op jit(solution)/shard_map/reverse
  59.9 0.2 fusion.12
  60.1 0.7 slice.13
  60.8 0.9 %slice.11 = f32[3,1,128,128]{2,3,0,1:T(8,128)S(1)} reverse(f32[3,1,128,128]{2,3,0,1:T(8,128)} %slice.13), dimensions={0} | reverse | bytes 393216 | tf_op jit(solution)/shard_map/slice | solution.py:58
  61.8 1.9 %fusion.4 = bf16[4,512,1,128]{1,3,0,2:T(8,128)(2,1)} fusion(f32[4,128,512]{2,1,0:T(8,128)S(1)} %copy-done.5, bf16[4,512,128]{2,1,0:T(8,128)(2,1)S(1)} %bitcast.91, f32[3,1,128,128]{2,3,0,1:T(8,128)S(1)} %slice.11, f32[128,128]{0,1:T(8,128)} %fusion.11), kind=kOutput, calls=%fused_computation.13 | convolution fusion | flops 67764224 | bytes 2359296 | tf_op jit(solution)/shard_map/bshd,bhde->bshe/dot_general | solution.py:71
  63.7 2.0 %copy.49 = bf16[4,512,1,128]{3,1,0,2:T(8,128)(2,1)} copy(bf16[4,512,1,128]{1,3,0,2:T(8,128)(2,1)} %fusion.4) | data formatting | bytes 1048576 | tf_op jit(solution)/shard_map/convert_element_type | solution.py:78
  65.8 1.7 %select_convert_fusion = bf16[4,512,512]{2,1,0:T(8,128)(2,1)S(1)} fusion(bf16[4,512,128]{2,1,0:T(8,128)(2,1)S(1)} %get-tuple-element.8, bf16[4,512,128]{2,1,0:T(8,128)(2,1)S(1)} %bitcast.87, pred[512,512]{1,0:T(8,128)(4,1)} %copy-done.9), kind=kOutput, calls=%fused_computation | convolution fusion | flops 270532608 | bytes 3407872 | tf_op jit(solution)/shard_map/bthe,bshe->bhts/dot_general | solution.py:60
  67.5 0.9 %convolution_bitcast_fusion = f32[4,128,512]{1,2,0:T(8,128)S(1)} fusion(bf16[4,512,512]{2,1,0:T(8,128)(2,1)S(1)} %select_convert_fusion, bf16[4,512,128]{2,1,0:T(8,128)(2,1)S(1)} %bitcast.83), kind=kOutput, calls=%fused_computation.2 | convolution fusion | flops 268435456 | bytes 3670016 | tf_op jit(solution)/shard_map/bhts,bthd->bshd/dot_general | solution.py:66
  68.4 1.1 %fusion.3 = bf16[4,128,512]{1,2,0:T(8,128)(2,1)} fusion(f32[4,128,512]{1,2,0:T(8,128)S(1)} %convolution_bitcast_fusion, bf16[4,512,128]{2,1,0:T(8,128)(2,1)S(1)} %bitcast.88, f32[3,1,128,128]{2,3,0,1:T(8,128)S(1)} %slice.11, f32[128,128]{0,1:T(8,128)S(1)} %copy-done.8), kind=kOutput, calls=%fused_computation.12 | convolution fusion | flops 67764224 | bytes 2359296 | tf_op jit(solution)/shard_map/bshe,bhde->bshd/dot_general | solution.py:67
  69.5 0.7 convolution_bitcast_fusion.1
  70.2 0.1 copy-done.7
  70.3 1.1 %fusion.1 = bf16[4,128,512]{1,2,0:T(8,128)(2,1)} fusion(f32[4,128,512]{1,2,0:T(8,128)S(1)} %convolution_bitcast_fusion.1, bf16[4,512,128]{2,1,0:T(8,128)(2,1)S(1)} %get-tuple-element.8, f32[3,1,128,128]{3,2,0,1:T(8,128)S(1)} %slice.12, f32[128,128]{1,0:T(8,128)S(1)} %copy-done.7), kind=kOutput, calls=%fused_computation.10 | convolution fusion | flops 67764224 | bytes 2359296 | tf_op jit(solution)/shard_map/bthe,bhde->bthd/dot_general | solution.py:63
  (22 shorter events, 0.1 us)
Async XLA Ops:
  0.6 1.0 %copy-start = (bf16[2048,128]{1,0:T(8,128)(2,1)S(1)}, bf16[2048,128]{1,0:T(8,128)(2,1)}, u32[]{:S(2)}) copy-start(bf16[2048,128]{1,0:T(8,128)(2,1)} %param.5) | copy-start | bytes 1572868
  0.6 3.0 %copy-start.1 = (bf16[2048,128]{1,0:T(8,128)(2,1)S(1)}, bf16[2048,128]{1,0:T(8,128)(2,1)}, u32[]{:S(2)}) copy-start(bf16[2048,128]{1,0:T(8,128)(2,1)} %param.7) | copy-start | bytes 1572868
  1.8 3.6 %copy-start.9 = (pred[512,512]{1,0:T(8,128)(4,1)}, pred[512,512]{1,0:T(8,128)(4,1)S(1)}, u32[]{:S(2)}) copy-start(pred[512,512]{1,0:T(8,128)(4,1)S(1)} %iota_compare_fusion) | copy-start | bytes 786436
  3.7 1.7 %copy-start.3 = (bf16[2048,128]{1,0:T(8,128)(2,1)S(1)}, bf16[2048,128]{1,0:T(8,128)(2,1)}, u32[]{:S(2)}) copy-start(bf16[2048,128]{1,0:T(8,128)(2,1)} %param.6) | copy-start | bytes 1572868
  5.4 14.5 %copy-start.10 = (f32[128]{0:T(128)S(1)}, f32[128]{0:T(128)}, u32[]{:S(2)}) copy-start(f32[128]{0:T(128)} %param.8) | copy-start | bytes 1540
  19.7 3.0 %copy-start.6 = (f32[128,128]{1,0:T(8,128)}, f32[128,128]{1,0:T(8,128)S(1)}, u32[]{:S(2)}) copy-start(f32[128,128]{1,0:T(8,128)S(1)} %copy.40) | copy-start | bytes 196612
  47.1 14.7 %copy-start.4 = (bf16[2048,128]{1,0:T(8,128)(2,1)S(1)}, bf16[2048,128]{1,0:T(8,128)(2,1)}, u32[]{:S(2)}) copy-start(bf16[2048,128]{1,0:T(8,128)(2,1)} %param.6) | copy-start | bytes 1572868
  47.1 14.7 %copy-start.5 = (f32[4,128,512]{2,1,0:T(8,128)S(1)}, f32[4,128,512]{2,1,0:T(8,128)}, u32[]{:S(2)}) copy-start(f32[4,128,512]{2,1,0:T(8,128)} %fusion.28) | copy-start | bytes 3145732
  60.1 5.6 %copy-start.2 = (bf16[2048,128]{1,0:T(8,128)(2,1)S(1)}, bf16[2048,128]{1,0:T(8,128)(2,1)}, u32[]{:S(2)}) copy-start(bf16[2048,128]{1,0:T(8,128)(2,1)} %param.7) | copy-start | bytes 1572868
  67.5 0.9 %copy-start.8 = (f32[128,128]{0,1:T(8,128)S(1)}, f32[128,128]{0,1:T(8,128)}, u32[]{:S(2)}) copy-start(f32[128,128]{0,1:T(8,128)} %fusion.11) | copy-start | bytes 196612
  69.5 0.8 %copy-start.7 = (f32[128,128]{1,0:T(8,128)S(1)}, f32[128,128]{1,0:T(8,128)}, u32[]{:S(2)}) copy-start(f32[128,128]{1,0:T(8,128)} %copy-done.6) | copy-start | bytes 196612
where the time goes:
time: 72 us; the launch traced here: 71.4 us
  blocking collectives  42.3 us (59%)
  matrix products  16.7 us (23%)
  local copies, waits for them, and re-layouts  7.31 us (10%)
  other arithmetic  4.29 us (6%)
  between operations  0.84 us (1%)
    psum x1, blocking collectives, body(): lax.psum((jnp.sum(output * output, (2, 3)), jnp.sum(scaled * output, (2,...  19 us
    all_gather x1, blocking collectives, body(): piece = lax.all_gather(totals[None], 'seq', axis=0, tiled=True)  12.4 us
    all_gather x1, blocking collectives, body(): piece = lax.all_gather(grad_total[None], 'seq', axis=0, tiled=True)  11 us
    another operation x1, other arithmetic  2.8 us
    dot_general x1, matrix products, body(): jnp.einsum('bthd,bhde->bthe', query4, prefix16, preferred_element_type=jn...  2.79 us
    convert_element_type x1, local copies, waits for them, and re-layouts, body(): value_grad.astype(jnp.bfloat16).reshape(tokens_here, -1)  2.04 us
    dot_general x1, matrix products, body(): jnp.einsum('bshd,bhde->bshe', key4, suffix16, preferred_element_type=jnp....  1.94 us
    dot_general x1, matrix products, body(): jnp.einsum('bthd,bshd->bhts', query4, key4, preferred_element_type=jnp.fl...  1.88 us

commit v1 on v0

v1 whole, which is shorter than its diff:
```python
import functools

import jax
import jax.numpy as jnp
from jax import lax
from jax.experimental import pallas as pl
from jax.experimental.pallas import tpu as pltpu
from jax.sharding import PartitionSpec as P

HEAD_DIM = 128
CHUNK = 256
EPS = 1e-05
MESH = pl.DeviceIdType.MESH
F32 = jnp.float32
BF16 = jnp.bfloat16


def dot(a, b, dim_a, dim_b):
    return lax.dot_general(a, b, (((dim_a,), (dim_b,)), ((), ())), preferred_element_type=F32)


def iota2(rows, columns):
    return (
        lax.broadcasted_iota(jnp.int32, (rows, columns), 0),
        lax.broadcasted_iota(jnp.int32, (rows, columns), 1),
    )


def exchange(total, pair_in, half_out, slots, half_acc, half_in, sems, chip, core, chips, upward):
    pair_s, pair_r, chip_s, chip_r, half_s, half_r = sems
    half = HEAD_DIM // 2
    mine = pl.ds(pl.multiple_of(core * half, half), half)
    partner = {"seq": chip * 2 + (1 - core)}

    def pair_copy():
        return pltpu.make_async_remote_copy(
            total, pair_in, pair_s, pair_r, device_id=partner, device_id_type=MESH
        )

    def chip_copy(slot, to):
        return pltpu.make_async_remote_copy(
            half_out, slots.at[slot], chip_s.at[to], chip_r.at[slot],
            device_id={"seq": to * 2 + core}, device_id_type=MESH,
        )

    def half_copy():
        return pltpu.make_async_remote_copy(
            half_acc, half_in, half_s, half_r, device_id=partner, device_id_type=MESH
        )

    def ahead(other):
        return (other > chip) if upward else (other < chip)

    def start_pair():
        pair_copy().start()

    def start_chips():
        pair_copy().wait_recv()
        half_out[...] = total[mine, :] + pair_in[mine, :]
        for step in range(1, chips):
            to = lax.rem(chip + step, chips)

            @pl.when(ahead(to))
            def _():
                chip_copy(chip, to).start()

    def start_halves():
        half_acc[...] = jnp.zeros_like(half_acc)
        for source in range(chips):

            @pl.when(jnp.logical_and(jnp.logical_not(ahead(source)), source != chip))
            def _():
                chip_copy(source, source).wait_recv()
                half_acc[...] += slots[source]

        half_copy().start()

    def finish(result):
        half_copy().wait_recv()
        result[mine, :] = half_acc[...]
        result[pl.ds(pl.multiple_of((1 - core) * half, half), half), :] = half_in[...]

        @pl.when(core == (1 if upward else 0))
        def _():
            result[...] += pair_in[...]

    def drain():
        pair_copy().wait_send()
        for to in range(chips):

            @pl.when(ahead(to))
            def _():
                chip_copy(chip, to).wait_send()

        half_copy().wait_send()

    return start_pair, start_chips, start_halves, finish, drain


def kernel(
    chips, heads, width_all,
    q_hbm, k_hbm, v_hbm, gain_ref, g_hbm,
    normed_hbm, qg_hbm, kg_hbm, vg_hbm,
    q, k, v, g, normed, qg, kg, vg,
    out32, attn_t, q_t, dout, prefix16, before, after, kpart, vpart,
    stats, stat_slots, scale_rows,
    total_f, pair_f, hout_f, slots_f, hacc_f, hin_f, earlier,
    total_b, pair_b, hout_b, slots_b, hacc_b, hin_b, later,
    in_sem, out_sem, stat_s, stat_r,
    pair_s, pair_r, chip_s, chip_r, half_s, half_r,
):
    seq_index = lax.axis_index("seq")
    head_index = lax.axis_index("head")
    chip = lax.div(seq_index, 2)
    core = lax.rem(seq_index, 2)
    tokens = q.shape[0]
    chunks = tokens // CHUNK
    groups = CHUNK // HEAD_DIM
    stat_rows = tokens // HEAD_DIM

    loads = [
        pltpu.make_async_copy(src, dst, in_sem.at[i])
        for i, (src, dst) in enumerate(((k_hbm, k), (v_hbm, v), (q_hbm, q), (g_hbm, g)))
    ]
    for load in loads:
        load.start()

    barrier = pltpu.get_barrier_semaphore()
    pl.semaphore_signal(
        barrier, inc=1, device_id={"seq": chip * 2 + (1 - core)}, device_id_type=MESH
    )
    for step in range(1, chips):
        pl.semaphore_signal(
            barrier, inc=1,
            device_id={"seq": lax.rem(chip + step, chips) * 2 + core}, device_id_type=MESH,
        )
    for step in range(1, heads):
        pl.semaphore_signal(
            barrier, inc=1, device_id={"head": lax.rem(head_index + step, heads)},
            device_id_type=MESH,
        )

    def rows(c):
        return pl.ds(pl.multiple_of(c * CHUNK, CHUNK), CHUNK)

    def sems(i):
        return (
            pair_s.at[i], pair_r.at[i], chip_s.at[i], chip_r.at[i], half_s.at[i], half_r.at[i]
        )

    forward = exchange(
        total_f, pair_f, hout_f, slots_f, hacc_f, hin_f, sems(0), chip, core, chips, True
    )
    backward = exchange(
        total_b, pair_b, hout_b, slots_b, hacc_b, hin_b, sems(1), chip, core, chips, False
    )

    loads[0].wait()
    loads[1].wait()
    running = jnp.zeros((HEAD_DIM, HEAD_DIM), F32)
    for c in range(chunks):
        before[c] = running
        running = running + dot(k[rows(c), :], v[rows(c), :], 0, 0)
    total_f[...] = running

    pl.semaphore_wait(barrier, 1 + (chips - 1) + (heads - 1))
    forward[0]()

    row, column = iota2(CHUNK, CHUNK)

    def local_output(c, carry):
        scores = dot(q[rows(c), :], k[rows(c), :], 1, 1)
        attn = jnp.where(row >= column, scores, 0.0).astype(BF16)
        out32[rows(c), :] = dot(attn, v[rows(c), :], 1, 0)
        return carry

    first = chunks // 4
    loads[2].wait()
    lax.fori_loop(0, first, local_output, 0, unroll=True)
    forward[1]()
    lax.fori_loop(first, chunks, local_output, 0, unroll=2)
    loads[3].wait()
    forward[2]()
    forward[3](earlier)

    eye_row, eye_column = iota2(HEAD_DIM, HEAD_DIM)
    eye = eye_row == eye_column
    gain = gain_ref[...]

    def finish_output(c, carry):
        prefix = (earlier[...] + before[c]).astype(BF16)
        prefix16[c] = prefix
        output = out32[rows(c), :] + dot(q[rows(c), :], prefix, 1, 0)
        out32[rows(c), :] = output
        scaled = g[rows(c), :].astype(F32) * gain
        square = jnp.sum(output * output, axis=1, keepdims=True)
        product = jnp.sum(scaled * output, axis=1, keepdims=True)
        for i in range(groups):
            part = slice(i * HEAD_DIM, (i + 1) * HEAD_DIM)
            stats[pl.ds(c * groups + i, 1), :] = jnp.sum(
                jnp.where(eye, square[part], 0.0), axis=0, keepdims=True
            )
            stats[pl.ds(stat_rows + c * groups + i, 1), :] = jnp.sum(
                jnp.where(eye, product[part], 0.0), axis=0, keepdims=True
            )
        return carry

    lax.fori_loop(0, chunks, finish_output, 0, unroll=2)

    def stat_copy(slot, to):
        return pltpu.make_async_remote_copy(
            stats, stat_slots.at[slot], stat_s.at[to], stat_r.at[slot],
            device_id={"head": to}, device_id_type=MESH,
        )

    for step in range(1, heads):
        to = lax.rem(head_index + step, heads)
        stat_copy(head_index, to).start()

    def transposed(c, carry):
        scores = dot(k[rows(c), :], q[rows(c), :], 1, 1)
        attn_t[c] = jnp.where(row <= column, scores, 0.0).astype(BF16)
        q_t[c] = q[rows(c), :].T
        return carry

    lax.fori_loop(0, chunks, transposed, 0, unroll=2)

    total = stats[...]
    for step in range(1, heads):
        source = lax.rem(head_index + step, heads)
        stat_copy(source, source).wait_recv()
        total = total + stat_slots[source]
    total = total * (1.0 / width_all)
    rstd = lax.rsqrt(total[:stat_rows] + EPS)
    scale_rows[:stat_rows] = rstd
    scale_rows[stat_rows:] = rstd * rstd * rstd * total[stat_rows:]

    def spread(r):
        return jnp.sum(jnp.where(eye, scale_rows[pl.ds(r, 1), :], 0.0), axis=1, keepdims=True)

    def columns(c, offset):
        return jnp.concatenate([spread(offset + c * groups + i) for i in range(groups)], axis=0)

    def gradient(i, running):
        c = chunks - 1 - i
        rstd_c = columns(c, 0)
        output = out32[rows(c), :]
        scaled = g[rows(c), :].astype(F32) * gain
        grad = (rstd_c * scaled - output * columns(c, stat_rows)).astype(BF16)
        dout[rows(c), :] = grad
        normed[rows(c), :] = (output * rstd_c * gain).astype(BF16)
        after[c] = running
        return running + dot(q_t[c], grad, 1, 0)

    total_b[...] = lax.fori_loop(
        0, chunks, gradient, jnp.zeros((HEAD_DIM, HEAD_DIM), F32), unroll=2
    )
    backward[0]()
    stores = [
        pltpu.make_async_copy(src, dst, out_sem.at[i])
        for i, (src, dst) in enumerate(
            ((normed, normed_hbm), (qg, qg_hbm), (kg, kg_hbm), (vg, vg_hbm))
        )
    ]
    stores[0].start()

    def local_gradients(c, carry):
        grad = dout[rows(c), :]
        value = v[rows(c), :]
        bmat = jnp.where(row >= column, dot(grad, value, 1, 1), 0.0).astype(BF16)
        bmat_t = jnp.where(row <= column, dot(value, grad, 1, 1), 0.0).astype(BF16)
        qg[rows(c), :] = (
            dot(bmat, k[rows(c), :], 1, 0) + dot(grad, prefix16[c], 1, 1)
        ).astype(BF16)
        kpart[rows(c), :] = dot(bmat_t, q[rows(c), :], 1, 0)
        vpart[rows(c), :] = dot(attn_t[c], grad, 1, 0)
        return carry

    lax.fori_loop(0, first, local_gradients, 0, unroll=True)
    backward[1]()
    lax.fori_loop(first, chunks, local_gradients, 0, unroll=2)
    stores[1].start()
    backward[2]()
    backward[3](later)

    def finish_gradients(c, carry):
        suffix = (later[...] + after[c]).astype(BF16)
        kg[rows(c), :] = (kpart[rows(c), :] + dot(v[rows(c), :], suffix, 1, 1)).astype(BF16)
        vg[rows(c), :] = (vpart[rows(c), :] + dot(k[rows(c), :], suffix, 1, 0)).astype(BF16)
        return carry

    lax.fori_loop(0, chunks, finish_gradients, 0, unroll=2)
    stores[2].start()
    stores[3].start()
    forward[4]()
    backward[4]()
    for step in range(1, heads):
        to = lax.rem(head_index + step, heads)
        stat_copy(head_index, to).wait_send()
    for store in stores:
        store.wait()


def body(queries, key_rows, value_rows, norm_gain, out_grad):
    tokens, width = queries.shape
    assert width == HEAD_DIM and tokens % CHUNK == 0
    chips = lax.axis_size("seq") // 2
    heads = lax.axis_size("head")
    chunks = tokens // CHUNK
    stat_rows = 2 * tokens // HEAD_DIM
    wide = (tokens, width)
    square = (HEAD_DIM, HEAD_DIM)
    half = (HEAD_DIM // 2, HEAD_DIM)
    link = [
        pltpu.VMEM(square, F32),
        pltpu.VMEM(square, F32),
        pltpu.VMEM(half, F32),
        pltpu.VMEM((chips,) + half, F32),
        pltpu.VMEM(half, F32),
        pltpu.VMEM(half, F32),
        pltpu.VMEM(square, F32),
    ]
    hbm = pl.BlockSpec(memory_space=pl.ANY)
    dma = pltpu.SemaphoreType.DMA
    return pl.pallas_call(
        functools.partial(kernel, chips, heads, width * heads),
        out_shape=[jax.ShapeDtypeStruct(wide, BF16)] * 4,
        in_specs=[hbm, hbm, hbm, pl.BlockSpec(memory_space=pltpu.VMEM), hbm],
        out_specs=[hbm] * 4,
        scratch_shapes=[pltpu.VMEM(wide, BF16)] * 8
        + [
            pltpu.VMEM(wide, F32),
            pltpu.VMEM((chunks, CHUNK, CHUNK), BF16),
            pltpu.VMEM((chunks, HEAD_DIM, CHUNK), BF16),
            pltpu.VMEM(wide, BF16),
            pltpu.VMEM((chunks,) + square, BF16),
            pltpu.VMEM((chunks,) + square, F32),
            pltpu.VMEM((chunks,) + square, F32),
            pltpu.VMEM(wide, F32),
            pltpu.VMEM(wide, F32),
            pltpu.VMEM((stat_rows, HEAD_DIM), F32),
            pltpu.VMEM((heads, stat_rows, HEAD_DIM), F32),
            pltpu.VMEM((stat_rows, HEAD_DIM), F32),
        ]
        + link
        + link
        + [
            dma((4,)), dma((4,)), dma((heads,)), dma((heads,)),
            dma((2,)), dma((2,)), dma((2, chips)), dma((2, chips)), dma((2,)), dma((2,)),
        ],
        compiler_params=pltpu.CompilerParams(
            collective_id=0, has_side_effects=True, vmem_limit_bytes=48 * 1024 * 1024
        ),
    )(queries, key_rows, value_rows, norm_gain.reshape(1, width), out_grad)


def solution(mesh):
    spec = P("seq", "head")
    return jax.shard_map(
        body,
        mesh=mesh,
        in_specs=(spec, spec, spec, P("head"), spec),
        out_specs=(spec,) * 4,
        check_vma=False,
    )
```

time: 72 us -> 34.1 us (0.47)
  blocking collectives: 42.3 us -> 0 us
  Pallas kernels: 0 us -> 25 us
  matrix products: 16.7 us -> 0 us
  other arithmetic: 4.29 us -> 0 us
    pallas_call x0 -> x1, Pallas kernels: none -> 25 us  [body(): pl.pallas_call(functools.partial(kernel, chips, heads, width * heads), ou...]
    all_gather x2 -> x0, blocking collectives: 23.3 us -> none  [the longest x1 12.4 us: body(): piece = lax.all_gather(totals[None], 'seq', axis=0, tiled=True)]
    psum x1 -> x0, blocking collectives: 19 us -> none  [body(): lax.psum((jnp.sum(output * output, (2, 3)), jnp.sum(scaled * output, (2,...]
    dot_general x12 -> x0, matrix products: 16.7 us -> none  [the longest x1 2.79 us: body(): jnp.einsum('bthd,bhde->bthe', query4, prefix16, preferred_element_type=jn...]
    unnamed x23 -> x14, local copies, waits for them, and re-layouts: 1.3 us -> 7.99 us
    another operation x3 -> x0, other arithmetic: 3.13 us -> none
    convert_element_type x1 -> x0, local copies, waits for them, and re-layouts: 2.04 us -> none  [body(): value_grad.astype(jnp.bfloat16).reshape(tokens_here, -1)]
    slice x3 -> x0, local copies, waits for them, and re-layouts: 1.64 us -> none  [the longest x2 1.63 us: body(): after = jnp.concatenate([behind[1:], jnp.zeros_like(grad_states[:1])], 0)]
where the time goes in v1:
time: 34.1 us; the launch traced here: 33.6 us
  Pallas kernels  25 us (73%)
  local copies, waits for them, and re-layouts  7.99 us (23%)
  between operations  0.65 us (2%)
    pallas_call x1, Pallas kernels, body(): pl.pallas_call(functools.partial(kernel, chips, heads, width * heads), ou...  25 us
    unnamed x14, local copies, waits for them, and re-layouts  7.99 us

profile of v1, /device:TPU:0, one launch (start us, length us, event | category | flops | bytes accessed | tf_op | source)
XLA Modules:
  0.0 33.6 jit_solution(15763820782638218014)
XLA Ops:
  0.6 0.0 copy-start.4
  0.6 0.6 %copy-done.4 = f32[128]{0:T(128)S(1)} copy-done((f32[128]{0:T(128)S(1)}, f32[128]{0:T(128)}, u32[]{:S(2)}) %copy-start.4) | copy-done | bytes 536
  1.3 0.0 copy-start
  1.3 1.0 %copy-done = bf16[2048,128]{1,0:T(8,128)(2,1)S(1)} copy-done((bf16[2048,128]{1,0:T(8,128)(2,1)S(1)}, bf16[2048,128]{1,0:T(8,128)(2,1)}, u32[]{:S(2)}) %copy-start) | copy-done | bytes 524312
  2.3 0.0 copy-start.1
  2.3 1.0 %copy-done.1 = bf16[2048,128]{1,0:T(8,128)(2,1)S(1)} copy-done((bf16[2048,128]{1,0:T(8,128)(2,1)S(1)}, bf16[2048,128]{1,0:T(8,128)(2,1)}, u32[]{:S(2)}) %copy-start.1) | copy-done | bytes 524312
  3.4 0.0 copy-start.2
  3.4 1.0 %copy-done.2 = bf16[2048,128]{1,0:T(8,128)(2,1)S(1)} copy-done((bf16[2048,128]{1,0:T(8,128)(2,1)S(1)}, bf16[2048,128]{1,0:T(8,128)(2,1)}, u32[]{:S(2)}) %copy-start.2) | copy-done | bytes 524312
  4.4 0.0 copy-start.3
  4.4 1.0 %copy-done.3 = bf16[2048,128]{1,0:T(8,128)(2,1)S(1)} copy-done((bf16[2048,128]{1,0:T(8,128)(2,1)S(1)}, bf16[2048,128]{1,0:T(8,128)(2,1)}, u32[]{:S(2)}) %copy-start.3) | copy-done | bytes 524312
  5.5 25.0 %shard_map.84 = (bf16[2048,128]{1,0:T(8,128)(2,1)S(1)}, bf16[2048,128]{1,0:T(8,128)(2,1)S(1)}, bf16[2048,128]{1,0:T(8,128)(2,1)S(1)}, bf16[2048,128]{1,0:T(8,128)(2,1)S(1)}) custom-call(bf16[2048,128]{1,0:T(8,128)(2,1)S(1)} %copy-done, bf16[2048,128]{1,0:T(8,128)(2,1)S(1)} %copy-done.1, bf16[2048,128]{1,0:T(8,128)(2,1)S(1)} %copy-done.2, ...), custom_call_target="tpu_custom_call" | custom-call | tf_op jit(solution)/shard_map/pallas_call | solution.py:325
  30.4 0.8 %copy.13 = bf16[2048,128]{1,0:T(8,128)(2,1)} copy(bf16[2048,128]{1,0:T(8,128)(2,1)S(1)} %get-tuple-element.8) | data formatting | bytes 1048576
  31.2 0.8 %copy.14 = bf16[2048,128]{1,0:T(8,128)(2,1)} copy(bf16[2048,128]{1,0:T(8,128)(2,1)S(1)} %get-tuple-element.9) | data formatting | bytes 1048576
  32.0 0.8 %copy.15 = bf16[2048,128]{1,0:T(8,128)(2,1)} copy(bf16[2048,128]{1,0:T(8,128)(2,1)S(1)} %get-tuple-element.10) | data formatting | bytes 1048576
  32.8 0.8 %copy.16 = bf16[2048,128]{1,0:T(8,128)(2,1)} copy(bf16[2048,128]{1,0:T(8,128)(2,1)S(1)} %get-tuple-element.11) | data formatting | bytes 1048576
Async XLA Ops:
  0.6 0.7 %copy-start.4 = (f32[128]{0:T(128)S(1)}, f32[128]{0:T(128)}, u32[]{:S(2)}) copy-start(f32[128]{0:T(128)} %param.8) | copy-start | bytes 1540
  1.3 1.0 %copy-start = (bf16[2048,128]{1,0:T(8,128)(2,1)S(1)}, bf16[2048,128]{1,0:T(8,128)(2,1)}, u32[]{:S(2)}) copy-start(bf16[2048,128]{1,0:T(8,128)(2,1)} %q_hbm.1) | copy-start | bytes 1572868
  2.3 1.0 %copy-start.1 = (bf16[2048,128]{1,0:T(8,128)(2,1)S(1)}, bf16[2048,128]{1,0:T(8,128)(2,1)}, u32[]{:S(2)}) copy-start(bf16[2048,128]{1,0:T(8,128)(2,1)} %k_hbm.1) | copy-start | bytes 1572868
  3.4 1.0 %copy-start.2 = (bf16[2048,128]{1,0:T(8,128)(2,1)S(1)}, bf16[2048,128]{1,0:T(8,128)(2,1)}, u32[]{:S(2)}) copy-start(bf16[2048,128]{1,0:T(8,128)(2,1)} %v_hbm.1) | copy-start | bytes 1572868
  4.4 1.0 %copy-start.3 = (bf16[2048,128]{1,0:T(8,128)(2,1)S(1)}, bf16[2048,128]{1,0:T(8,128)(2,1)}, u32[]{:S(2)}) copy-start(bf16[2048,128]{1,0:T(8,128)(2,1)} %g_hbm.1) | copy-start | bytes 1572868

commit v2 on v1

--- a/solution.py
+++ b/solution.py
@@ -99,14 +99,14 @@
 
 def kernel(
     chips, heads, width_all,
-    q_hbm, k_hbm, v_hbm, gain_ref, g_hbm,
-    normed_hbm, qg_hbm, kg_hbm, vg_hbm,
-    q, k, v, g, normed, qg, kg, vg,
-    out32, attn_t, q_t, dout, prefix16, before, after, kpart, vpart,
+    q_hbm, k_hbm, v_hbm, gain_hbm, g_hbm,
+    normed, qg, kpart, vpart, suffix16, k, v,
+    q, g, gain_ref,
+    out32, attn_t, q_t, dout, prefix16, before, after,
     stats, stat_slots, scale_rows,
     total_f, pair_f, hout_f, slots_f, hacc_f, hin_f, earlier,
     total_b, pair_b, hout_b, slots_b, hacc_b, hin_b, later,
-    in_sem, out_sem, stat_s, stat_r,
+    in_sem, stat_s, stat_r,
     pair_s, pair_r, chip_s, chip_r, half_s, half_r,
 ):
     seq_index = lax.axis_index("seq")
@@ -120,7 +120,9 @@
 
     loads = [
         pltpu.make_async_copy(src, dst, in_sem.at[i])
-        for i, (src, dst) in enumerate(((k_hbm, k), (v_hbm, v), (q_hbm, q), (g_hbm, g)))
+        for i, (src, dst) in enumerate(
+            ((k_hbm, k), (v_hbm, v), (q_hbm, q), (g_hbm, g), (gain_hbm, gain_ref))
+        )
     ]
     for load in loads:
         load.start()
@@ -180,6 +182,7 @@
     forward[1]()
     lax.fori_loop(first, chunks, local_output, 0, unroll=2)
     loads[3].wait()
+    loads[4].wait()
     forward[2]()
     forward[3](earlier)
 
@@ -256,14 +259,6 @@
         0, chunks, gradient, jnp.zeros((HEAD_DIM, HEAD_DIM), F32), unroll=2
     )
     backward[0]()
-    stores = [
-        pltpu.make_async_copy(src, dst, out_sem.at[i])
-        for i, (src, dst) in enumerate(
-            ((normed, normed_hbm), (qg, qg_hbm), (kg, kg_hbm), (vg, vg_hbm))
-        )
-    ]
-    stores[0].start()
-
     def local_gradients(c, carry):
         grad = dout[rows(c), :]
         value = v[rows(c), :]
@@ -279,24 +274,44 @@
     lax.fori_loop(0, first, local_gradients, 0, unroll=True)
     backward[1]()
     lax.fori_loop(first, chunks, local_gradients, 0, unroll=2)
-    stores[1].start()
     backward[2]()
     backward[3](later)
-
-    def finish_gradients(c, carry):
-        suffix = (later[...] + after[c]).astype(BF16)
-        kg[rows(c), :] = (kpart[rows(c), :] + dot(v[rows(c), :], suffix, 1, 1)).astype(BF16)
-        vg[rows(c), :] = (vpart[rows(c), :] + dot(k[rows(c), :], suffix, 1, 0)).astype(BF16)
-        return carry
-
-    lax.fori_loop(0, chunks, finish_gradients, 0, unroll=2)
-    stores[2].start()
-    stores[3].start()
+    for c in range(chunks):
+        suffix16[c] = (later[...] + after[c]).astype(BF16)
     forward[4]()
     backward[4]()
     for step in range(1, heads):
         to = lax.rem(head_index + step, heads)
         stat_copy(head_index, to).wait_send()
+
+
+def last_kernel(
+    normed, qg, kpart, vpart, suffix16, k, v, normed_hbm, qg_hbm, kg_hbm, vg_hbm, kg, vg, sem
+):
+    chunks = k.shape[0] // CHUNK
+    parts = 2 if chunks % 2 == 0 else 1
+    per_part = chunks // parts
+    stores = [
+        pltpu.make_async_copy(normed, normed_hbm, sem.at[0]),
+        pltpu.make_async_copy(qg, qg_hbm, sem.at[1]),
+    ]
+    for store in stores:
+        store.start()
+
+    def finish_gradients(c, carry):
+        part = pl.ds(pl.multiple_of(c * CHUNK, CHUNK), CHUNK)
+        suffix = suffix16[c]
+        kg[part, :] = (kpart[part, :] + dot(v[part, :], suffix, 1, 1)).astype(BF16)
+        vg[part, :] = (vpart[part, :] + dot(k[part, :], suffix, 1, 0)).astype(BF16)
+        return carry
+
+    for i in range(parts):
+        lax.fori_loop(i * per_part, (i + 1) * per_part, finish_gradients, 0, unroll=2)
+        part = pl.ds(i * per_part * CHUNK, per_part * CHUNK)
+        for n, (src, dst) in enumerate(((kg, kg_hbm), (vg, vg_hbm))):
+            store = pltpu.make_async_copy(src.at[part], dst.at[part], sem.at[2 + 2 * i + n])
+            store.start()
+            stores.append(store)
     for store in stores:
         store.wait()
 
@@ -320,15 +335,26 @@
         pltpu.VMEM(half, F32),
         pltpu.VMEM(square, F32),
     ]
-    hbm = pl.BlockSpec(memory_space=pl.ANY)
+    hbm = pl.BlockSpec(memory_space=pltpu.HBM)
+    vmem = pl.BlockSpec(memory_space=pltpu.VMEM)
     dma = pltpu.SemaphoreType.DMA
-    return pl.pallas_call(
+    held = pl.pallas_call(
         functools.partial(kernel, chips, heads, width * heads),
-        out_shape=[jax.ShapeDtypeStruct(wide, BF16)] * 4,
-        in_specs=[hbm, hbm, hbm, pl.BlockSpec(memory_space=pltpu.VMEM), hbm],
-        out_specs=[hbm] * 4,
-        scratch_shapes=[pltpu.VMEM(wide, BF16)] * 8
-        + [
+        out_shape=[
+            jax.ShapeDtypeStruct(wide, BF16),
+            jax.ShapeDtypeStruct(wide, BF16),
+            jax.ShapeDtypeStruct(wide, F32),
+            jax.ShapeDtypeStruct(wide, F32),
+            jax.ShapeDtypeStruct((chunks,) + square, BF16),
+            jax.ShapeDtypeStruct(wide, BF16),
+            jax.ShapeDtypeStruct(wide, BF16),
+        ],
+        in_specs=[hbm] * 5,
+        out_specs=[vmem] * 7,
+        scratch_shapes=[
+            pltpu.VMEM(wide, BF16),
+            pltpu.VMEM(wide, BF16),
+            pltpu.VMEM((1, width), F32),
             pltpu.VMEM(wide, F32),
             pltpu.VMEM((chunks, CHUNK, CHUNK), BF16),
             pltpu.VMEM((chunks, HEAD_DIM, CHUNK), BF16),
@@ -336,8 +362,6 @@
             pltpu.VMEM((chunks,) + square, BF16),
             pltpu.VMEM((chunks,) + square, F32),
             pltpu.VMEM((chunks,) + square, F32),
-            pltpu.VMEM(wide, F32),
-            pltpu.VMEM(wide, F32),
             pltpu.VMEM((stat_rows, HEAD_DIM), F32),
             pltpu.VMEM((heads, stat_rows, HEAD_DIM), F32),
             pltpu.VMEM((stat_rows, HEAD_DIM), F32),
@@ -345,13 +369,24 @@
         + link
         + link
         + [
-            dma((4,)), dma((4,)), dma((heads,)), dma((heads,)),
+            dma((5,)), dma((heads,)), dma((heads,)),
             dma((2,)), dma((2,)), dma((2, chips)), dma((2, chips)), dma((2,)), dma((2,)),
         ],
         compiler_params=pltpu.CompilerParams(
-            collective_id=0, has_side_effects=True, vmem_limit_bytes=48 * 1024 * 1024
+            collective_id=0, has_side_effects=True, vmem_limit_bytes=32 * 1024 * 1024
         ),
-    )(queries, key_rows, value_rows, norm_gain.reshape(1, width), out_grad)
+    )(*[
+        pltpu.with_memory_space_constraint(array, pltpu.HBM)
+        for array in (queries, key_rows, value_rows, norm_gain.reshape(1, width), out_grad)
+    ])
+    return pl.pallas_call(
+        last_kernel,
+        out_shape=[jax.ShapeDtypeStruct(wide, BF16)] * 4,
+        in_specs=[vmem] * 7,
+        out_specs=[hbm] * 4,
+        scratch_shapes=[pltpu.VMEM(wide, BF16), pltpu.VMEM(wide, BF16), dma((6,))],
+        compiler_params=pltpu.CompilerParams(vmem_limit_bytes=32 * 1024 * 1024),
+    )(*held)
 
 
 def solution(mesh):

time: 34.1 us -> 26.6 us (0.78); the launches traced: 33.6 us -> 26.5 us
  local copies, waits for them, and re-layouts: 7.99 us -> 0 us
  Pallas kernels: 25 us -> 25.8 us
    unnamed x14 -> x0, local copies, waits for them, and re-layouts: 7.99 us -> none
    pallas_call x0 -> x1, Pallas kernels: none -> 1.73 us  [body(): pl.pallas_call(last_kernel, out_shape=[jax.ShapeDtypeStruct(wide, BF16)]...]
    pallas_call x1, Pallas kernels: 25 us -> 24.1 us  [body(): pl.pallas_call(functools.partial(kernel, chips, heads, width * heads), ou...]
where the time goes in v2:
time: 26.6 us; the launch traced here: 26.5 us
  Pallas kernels  25.8 us (97%)
  between operations  0.64 us (2%)
    pallas_call x1, Pallas kernels, body(): pl.pallas_call(functools.partial(kernel, chips, heads, width * heads), ou...  24.1 us
    pallas_call x1, Pallas kernels, body(): pl.pallas_call(last_kernel, out_shape=[jax.ShapeDtypeStruct(wide, BF16)]...  1.73 us

profile of v2, /device:TPU:0, one launch (start us, length us, event | category | flops | bytes accessed | tf_op | source)
XLA Modules:
  0.0 26.5 jit_solution(10507861913628780045)
XLA Ops:
  0.6 24.1 %shard_map.84 = (bf16[2048,128]{1,0:T(8,128)(2,1)S(1)}, bf16[2048,128]{1,0:T(8,128)(2,1)S(1)}, f32[2048,128]{1,0:T(8,128)S(1)}, f32[2048,128]{1,0:T(8,128)S(1)},...) custom-call(bf16[2048,128]{1,0:T(8,128)(2,1)} %q_hbm.1, ...), custom_call_target="tpu_custom_call" | custom-call | tf_op jit(solution)/shard_map/pallas_call | solution.py:341
  24.8 1.7 %shard_map.85 = (bf16[2048,128]{1,0:T(8,128)(2,1)}, bf16[2048,128]{1,0:T(8,128)(2,1)}, bf16[2048,128]{1,0:T(8,128)(2,1)}, bf16[2048,128]{1,0:T(8,128)(2,1)}) custom-call(bf16[2048,128]{1,0:T(8,128)(2,1)S(1)} %get-tuple-element.11.normed, bf16[2048,128]{1,0:T(8,128)(2,1)S(1)} %get-tuple-element.12.qg, f32[2048,128]{1,0:T(8,128)S(1)} %get-tuple-element.13.kpart, ...), custom_call_target="tpu_custom_call" | custom-call | tf_op jit(solution)/shard_map/pallas_call | solution.py:382

commit v3 on v2

--- a/solution.py
+++ b/solution.py
@@ -9,6 +9,8 @@
 
 HEAD_DIM = 128
 CHUNK = 256
+PIECES = 2
+UNROLL = 4
 EPS = 1e-05
 MESH = pl.DeviceIdType.MESH
 F32 = jnp.float32
@@ -100,9 +102,9 @@
 def kernel(
     chips, heads, width_all,
     q_hbm, k_hbm, v_hbm, gain_hbm, g_hbm,
-    normed, qg, kpart, vpart, suffix16, k, v,
+    normed, qg, kpart, vpart, later16, k, v,
     q, g, gain_ref,
-    out32, attn_t, q_t, dout, prefix16, before, after,
+    out32, attn_t, q_t, dout, before, after,
     stats, stat_slots, scale_rows,
     total_f, pair_f, hout_f, slots_f, hacc_f, hin_f, earlier,
     total_b, pair_b, hout_b, slots_b, hacc_b, hin_b, later,
@@ -116,7 +118,8 @@
     tokens = q.shape[0]
     chunks = tokens // CHUNK
     groups = CHUNK // HEAD_DIM
-    stat_rows = tokens // HEAD_DIM
+    per_piece = chunks // PIECES
+    stat_rows = per_piece * groups
 
     loads = [
         pltpu.make_async_copy(src, dst, in_sem.at[i])
@@ -173,7 +176,9 @@
     def local_output(c, carry):
         scores = dot(q[rows(c), :], k[rows(c), :], 1, 1)
         attn = jnp.where(row >= column, scores, 0.0).astype(BF16)
-        out32[rows(c), :] = dot(attn, v[rows(c), :], 1, 0)
+        out32[rows(c), :] = dot(attn, v[rows(c), :], 1, 0) + dot(
+            q[rows(c), :], before[c].astype(BF16), 1, 0
+        )
         return carry
 
     first = chunks // 4
@@ -181,44 +186,6 @@
     lax.fori_loop(0, first, local_output, 0, unroll=True)
     forward[1]()
     lax.fori_loop(first, chunks, local_output, 0, unroll=2)
-    loads[3].wait()
-    loads[4].wait()
-    forward[2]()
-    forward[3](earlier)
-
-    eye_row, eye_column = iota2(HEAD_DIM, HEAD_DIM)
-    eye = eye_row == eye_column
-    gain = gain_ref[...]
-
-    def finish_output(c, carry):
-        prefix = (earlier[...] + before[c]).astype(BF16)
-        prefix16[c] = prefix
-        output = out32[rows(c), :] + dot(q[rows(c), :], prefix, 1, 0)
-        out32[rows(c), :] = output
-        scaled = g[rows(c), :].astype(F32) * gain
-        square = jnp.sum(output * output, axis=1, keepdims=True)
-        product = jnp.sum(scaled * output, axis=1, keepdims=True)
-        for i in range(groups):
-            part = slice(i * HEAD_DIM, (i + 1) * HEAD_DIM)
-            stats[pl.ds(c * groups + i, 1), :] = jnp.sum(
-                jnp.where(eye, square[part], 0.0), axis=0, keepdims=True
-            )
-            stats[pl.ds(stat_rows + c * groups + i, 1), :] = jnp.sum(
-                jnp.where(eye, product[part], 0.0), axis=0, keepdims=True
-            )
-        return carry
-
-    lax.fori_loop(0, chunks, finish_output, 0, unroll=2)
-
-    def stat_copy(slot, to):
-        return pltpu.make_async_remote_copy(
-            stats, stat_slots.at[slot], stat_s.at[to], stat_r.at[slot],
-            device_id={"head": to}, device_id_type=MESH,
-        )
-
-    for step in range(1, heads):
-        to = lax.rem(head_index + step, heads)
-        stat_copy(head_index, to).start()
 
     def transposed(c, carry):
         scores = dot(k[rows(c), :], q[rows(c), :], 1, 1)
@@ -227,48 +194,101 @@
         return carry
 
     lax.fori_loop(0, chunks, transposed, 0, unroll=2)
-
-    total = stats[...]
-    for step in range(1, heads):
-        source = lax.rem(head_index + step, heads)
-        stat_copy(source, source).wait_recv()
-        total = total + stat_slots[source]
-    total = total * (1.0 / width_all)
-    rstd = lax.rsqrt(total[:stat_rows] + EPS)
-    scale_rows[:stat_rows] = rstd
-    scale_rows[stat_rows:] = rstd * rstd * rstd * total[stat_rows:]
-
-    def spread(r):
-        return jnp.sum(jnp.where(eye, scale_rows[pl.ds(r, 1), :], 0.0), axis=1, keepdims=True)
-
-    def columns(c, offset):
-        return jnp.concatenate([spread(offset + c * groups + i) for i in range(groups)], axis=0)
-
-    def gradient(i, running):
-        c = chunks - 1 - i
-        rstd_c = columns(c, 0)
-        output = out32[rows(c), :]
-        scaled = g[rows(c), :].astype(F32) * gain
-        grad = (rstd_c * scaled - output * columns(c, stat_rows)).astype(BF16)
-        dout[rows(c), :] = grad
-        normed[rows(c), :] = (output * rstd_c * gain).astype(BF16)
-        after[c] = running
-        return running + dot(q_t[c], grad, 1, 0)
-
-    total_b[...] = lax.fori_loop(
-        0, chunks, gradient, jnp.zeros((HEAD_DIM, HEAD_DIM), F32), unroll=2
-    )
+    loads[3].wait()
+    loads[4].wait()
+    forward[2]()
+    forward[3](earlier)
+
+    eye_row, eye_column = iota2(HEAD_DIM, HEAD_DIM)
+    eye = eye_row == eye_column
+    gain = gain_ref[...]
+    earlier16 = earlier[...].astype(BF16)
+
+    def stat_copy(piece, slot, to):
+        return pltpu.make_async_remote_copy(
+            stats.at[piece], stat_slots.at[piece, slot],
+            stat_s.at[piece, to], stat_r.at[piece, slot],
+            device_id={"head": to}, device_id_type=MESH,
+        )
+
+    for piece in reversed(range(PIECES)):
+
+        def finish_output(i, carry, piece=piece):
+            c = piece * per_piece + i
+            output = out32[rows(c), :] + dot(q[rows(c), :], earlier16, 1, 0)
+            out32[rows(c), :] = output
+            scaled = g[rows(c), :].astype(F32) * gain
+            square = jnp.sum(output * output, axis=1, keepdims=True)
+            product = jnp.sum(scaled * output, axis=1, keepdims=True)
+            for n in range(groups):
+                part = slice(n * HEAD_DIM, (n + 1) * HEAD_DIM)
+                stats[piece, pl.ds(i * groups + n, 1), :] = jnp.sum(
+                    jnp.where(eye, square[part], 0.0), axis=0, keepdims=True
+                )
+                stats[piece, pl.ds(stat_rows + i * groups + n, 1), :] = jnp.sum(
+                    jnp.where(eye, product[part], 0.0), axis=0, keepdims=True
+                )
+            return carry
+
+        lax.fori_loop(0, per_piece, finish_output, 0, unroll=UNROLL)
+        for step in range(1, heads):
+            to = lax.rem(head_index + step, heads)
+            stat_copy(piece, head_index, to).start()
+
+    running = jnp.zeros((HEAD_DIM, HEAD_DIM), F32)
+    for piece in reversed(range(PIECES)):
+        total = stats[piece]
+        for step in range(1, heads):
+            source = lax.rem(head_index + step, heads)
+            stat_copy(piece, source, source).wait_recv()
+            total = total + stat_slots[piece, source]
+        total = total * (1.0 / width_all)
+        rstd = lax.rsqrt(total[:stat_rows] + EPS)
+        scale_rows[piece, :stat_rows] = rstd
+        scale_rows[piece, stat_rows:] = rstd * rstd * rstd * total[stat_rows:]
+
+        def gradient(i, running, piece=piece):
+            def columns(offset):
+                return jnp.concatenate(
+                    [
+                        jnp.sum(
+                            jnp.where(eye, scale_rows[piece, pl.ds(offset + n, 1), :], 0.0),
+                            axis=1, keepdims=True,
+                        )
+                        for n in range(groups)
+                    ],
+                    axis=0,
+                )
+
+            at = per_piece - 1 - i
+            c = piece * per_piece + at
+            rstd_c = columns(at * groups)
+            output = out32[rows(c), :]
+            scaled = g[rows(c), :].astype(F32) * gain
+            grad = (rstd_c * scaled - output * columns(stat_rows + at * groups)).astype(BF16)
+            dout[rows(c), :] = grad
+            out32[rows(c), :] = output * rstd_c
+            after[c] = running
+            return running + dot(q_t[c], grad, 1, 0)
+
+        running = lax.fori_loop(0, per_piece, gradient, running, unroll=UNROLL)
+
+    total_b[...] = running
     backward[0]()
+
     def local_gradients(c, carry):
         grad = dout[rows(c), :]
         value = v[rows(c), :]
+        prefix = (earlier[...] + before[c]).astype(BF16)
+        suffix = after[c].astype(BF16)
         bmat = jnp.where(row >= column, dot(grad, value, 1, 1), 0.0).astype(BF16)
         bmat_t = jnp.where(row <= column, dot(value, grad, 1, 1), 0.0).astype(BF16)
         qg[rows(c), :] = (
-            dot(bmat, k[rows(c), :], 1, 0) + dot(grad, prefix16[c], 1, 1)
+            dot(bmat, k[rows(c), :], 1, 0) + dot(grad, prefix, 1, 1)
         ).astype(BF16)
-        kpart[rows(c), :] = dot(bmat_t, q[rows(c), :], 1, 0)
-        vpart[rows(c), :] = dot(attn_t[c], grad, 1, 0)
+        kpart[rows(c), :] = dot(bmat_t, q[rows(c), :], 1, 0) + dot(value, suffix, 1, 1)
+        vpart[rows(c), :] = dot(attn_t[c], grad, 1, 0) + dot(k[rows(c), :], suffix, 1, 0)
+        normed[rows(c), :] = (out32[rows(c), :] * gain).astype(BF16)
         return carry
 
     lax.fori_loop(0, first, local_gradients, 0, unroll=True)
@@ -276,20 +296,20 @@
     lax.fori_loop(first, chunks, local_gradients, 0, unroll=2)
     backward[2]()
     backward[3](later)
-    for c in range(chunks):
-        suffix16[c] = (later[...] + after[c]).astype(BF16)
+    later16[...] = later[...].astype(BF16)
     forward[4]()
     backward[4]()
-    for step in range(1, heads):
-        to = lax.rem(head_index + step, heads)
-        stat_copy(head_index, to).wait_send()
+    for piece in range(PIECES):
+        for step in range(1, heads):
+            to = lax.rem(head_index + step, heads)
+            stat_copy(piece, head_index, to).wait_send()
 
 
 def last_kernel(
-    normed, qg, kpart, vpart, suffix16, k, v, normed_hbm, qg_hbm, kg_hbm, vg_hbm, kg, vg, sem
+    normed, qg, kpart, vpart, later16, k, v, normed_hbm, qg_hbm, kg_hbm, vg_hbm, kg, vg, sem
 ):
     chunks = k.shape[0] // CHUNK
-    parts = 2 if chunks % 2 == 0 else 1
+    parts = 4 if chunks % 4 == 0 else 1
     per_part = chunks // parts
     stores = [
         pltpu.make_async_copy(normed, normed_hbm, sem.at[0]),
@@ -298,9 +318,10 @@
     for store in stores:
         store.start()
 
+    suffix = later16[...]
+
     def finish_gradients(c, carry):
         part = pl.ds(pl.multiple_of(c * CHUNK, CHUNK), CHUNK)
-        suffix = suffix16[c]
         kg[part, :] = (kpart[part, :] + dot(v[part, :], suffix, 1, 1)).astype(BF16)
         vg[part, :] = (vpart[part, :] + dot(k[part, :], suffix, 1, 0)).astype(BF16)
         return carry
@@ -322,7 +343,7 @@
     chips = lax.axis_size("seq") // 2
     heads = lax.axis_size("head")
     chunks = tokens // CHUNK
-    stat_rows = 2 * tokens // HEAD_DIM
+    stat_rows = 2 * tokens // HEAD_DIM // PIECES
     wide = (tokens, width)
     square = (HEAD_DIM, HEAD_DIM)
     half = (HEAD_DIM // 2, HEAD_DIM)
@@ -345,7 +366,7 @@
             jax.ShapeDtypeStruct(wide, BF16),
             jax.ShapeDtypeStruct(wide, F32),
             jax.ShapeDtypeStruct(wide, F32),
-            jax.ShapeDtypeStruct((chunks,) + square, BF16),
+            jax.ShapeDtypeStruct(square, BF16),
             jax.ShapeDtypeStruct(wide, BF16),
             jax.ShapeDtypeStruct(wide, BF16),
         ],
@@ -359,17 +380,16 @@
             pltpu.VMEM((chunks, CHUNK, CHUNK), BF16),
             pltpu.VMEM((chunks, HEAD_DIM, CHUNK), BF16),
             pltpu.VMEM(wide, BF16),
-            pltpu.VMEM((chunks,) + square, BF16),
             pltpu.VMEM((chunks,) + square, F32),
             pltpu.VMEM((chunks,) + square, F32),
-            pltpu.VMEM((stat_rows, HEAD_DIM), F32),
-            pltpu.VMEM((heads, stat_rows, HEAD_DIM), F32),
-            pltpu.VMEM((stat_rows, HEAD_DIM), F32),
+            pltpu.VMEM((PIECES, stat_rows, HEAD_DIM), F32),
+            pltpu.VMEM((PIECES, heads, stat_rows, HEAD_DIM), F32),
+            pltpu.VMEM((PIECES, stat_rows, HEAD_DIM), F32),
         ]
         + link
         + link
         + [
-            dma((5,)), dma((heads,)), dma((heads,)),
+            dma((5,)), dma((PIECES, heads)), dma((PIECES, heads)),
             dma((2,)), dma((2,)), dma((2, chips)), dma((2, chips)), dma((2,)), dma((2,)),
         ],
         compiler_params=pltpu.CompilerParams(
@@ -384,7 +404,7 @@
         out_shape=[jax.ShapeDtypeStruct(wide, BF16)] * 4,
         in_specs=[vmem] * 7,
         out_specs=[hbm] * 4,
-        scratch_shapes=[pltpu.VMEM(wide, BF16), pltpu.VMEM(wide, BF16), dma((6,))],
+        scratch_shapes=[pltpu.VMEM(wide, BF16), pltpu.VMEM(wide, BF16), dma((10,))],
         compiler_params=pltpu.CompilerParams(vmem_limit_bytes=32 * 1024 * 1024),
     )(*held)
 

time: 26.6 us -> 24.7 us (0.929)
  Pallas kernels: 25.8 us -> 23.9 us
    pallas_call x1, Pallas kernels: 24.1 us -> 22.5 us  [body(): pl.pallas_call(functools.partial(kernel, chips, heads, width * heads), ou...]
    pallas_call x1, Pallas kernels: 1.73 us -> 1.39 us  [body(): pl.pallas_call(last_kernel, out_shape=[jax.ShapeDtypeStruct(wide, BF16)]...]
where the time goes in v3:
time: 24.7 us; the launch traced here: 24.5 us
  Pallas kernels  23.9 us (97%)
  between operations  0.64 us (3%)
    pallas_call x1, Pallas kernels, body(): pl.pallas_call(functools.partial(kernel, chips, heads, width * heads), ou...  22.5 us
    pallas_call x1, Pallas kernels, body(): pl.pallas_call(last_kernel, out_shape=[jax.ShapeDtypeStruct(wide, BF16)]...  1.39 us

profile of v3, /device:TPU:0, one launch (start us, length us, event | category | flops | bytes accessed | tf_op | source)
XLA Modules:
  0.0 24.5 jit_solution(14655745617265154300)
XLA Ops:
  0.6 22.5 %shard_map.84 = (bf16[2048,128]{1,0:T(8,128)(2,1)S(1)}, bf16[2048,128]{1,0:T(8,128)(2,1)S(1)}, f32[2048,128]{1,0:T(8,128)S(1)}, f32[2048,128]{1,0:T(8,128)S(1)},...) custom-call(bf16[2048,128]{1,0:T(8,128)(2,1)} %q_hbm.1, ...), custom_call_target="tpu_custom_call" | custom-call | tf_op jit(solution)/shard_map/pallas_call | solution.py:362
  23.2 1.4 %shard_map.85 = (bf16[2048,128]{1,0:T(8,128)(2,1)}, bf16[2048,128]{1,0:T(8,128)(2,1)}, bf16[2048,128]{1,0:T(8,128)(2,1)}, bf16[2048,128]{1,0:T(8,128)(2,1)}) custom-call(bf16[2048,128]{1,0:T(8,128)(2,1)S(1)} %get-tuple-element.11.normed, bf16[2048,128]{1,0:T(8,128)(2,1)S(1)} %get-tuple-element.12.qg, f32[2048,128]{1,0:T(8,128)S(1)} %get-tuple-element.13.kpart, ...), custom_call_target="tpu_custom_call" | custom-call | tf_op jit(solution)/shard_map/pallas_call | solution.py:402

commit v4 on v3

--- a/solution.py
+++ b/solution.py
@@ -11,6 +11,7 @@
 CHUNK = 256
 PIECES = 2
 UNROLL = 4
+SHARE = 32
 EPS = 1e-05
 MESH = pl.DeviceIdType.MESH
 F32 = jnp.float32
@@ -30,8 +31,12 @@
 
 def exchange(total, pair_in, half_out, slots, half_acc, half_in, sems, chip, core, chips, upward):
     pair_s, pair_r, chip_s, chip_r, half_s, half_r = sems
-    half = HEAD_DIM // 2
-    mine = pl.ds(pl.multiple_of(core * half, half), half)
+    share = half_out.shape[0]
+    rest = pl.ds(2 * share, HEAD_DIM - 2 * share)
+    slot_share = pl.ds(0, share)
+    slot_rest = pl.ds(share, HEAD_DIM - 2 * share)
+    mine = pl.ds(pl.multiple_of(core * share, share), share)
+    others = pl.ds(pl.multiple_of((1 - core) * share, share), share)
     partner = {"seq": chip * 2 + (1 - core)}
 
     def pair_copy():
@@ -39,9 +44,15 @@
             total, pair_in, pair_s, pair_r, device_id=partner, device_id_type=MESH
         )
 
-    def chip_copy(slot, to):
+    def share_copy(slot, to):
         return pltpu.make_async_remote_copy(
-            half_out, slots.at[slot], chip_s.at[to], chip_r.at[slot],
+            half_out, slots.at[slot, slot_share], chip_s.at[to, 0], chip_r.at[slot, 0],
+            device_id={"seq": to * 2 + core}, device_id_type=MESH,
+        )
+
+    def rest_copy(slot, to):
+        return pltpu.make_async_remote_copy(
+            total.at[rest], slots.at[slot, slot_rest], chip_s.at[to, 1], chip_r.at[slot, 1],
             device_id={"seq": to * 2 + core}, device_id_type=MESH,
         )
 
@@ -55,6 +66,12 @@
 
     def start_pair():
         pair_copy().start()
+        for step in range(1, chips):
+            to = lax.rem(chip + step, chips)
+
+            @pl.when(ahead(to))
+            def _():
+                rest_copy(chip, to).start()
 
     def start_chips():
         pair_copy().wait_recv()
@@ -64,7 +81,7 @@
 
             @pl.when(ahead(to))
             def _():
-                chip_copy(chip, to).start()
+                share_copy(chip, to).start()
 
     def start_halves():
         half_acc[...] = jnp.zeros_like(half_acc)
@@ -72,15 +89,17 @@
 
             @pl.when(jnp.logical_and(jnp.logical_not(ahead(source)), source != chip))
             def _():
-                chip_copy(source, source).wait_recv()
+                rest_copy(source, source).wait_recv()
+                share_copy(source, source).wait_recv()
                 half_acc[...] += slots[source]
 
         half_copy().start()
 
     def finish(result):
         half_copy().wait_recv()
-        result[mine, :] = half_acc[...]
-        result[pl.ds(pl.multiple_of((1 - core) * half, half), half), :] = half_in[...]
+        result[mine, :] = half_acc[slot_share, :]
+        result[others, :] = half_in[slot_share, :]
+        result[rest, :] = half_acc[slot_rest, :] + half_in[slot_rest, :]
 
         @pl.when(core == (1 if upward else 0))
         def _():
@@ -92,7 +111,8 @@
 
             @pl.when(ahead(to))
             def _():
-                chip_copy(chip, to).wait_send()
+                rest_copy(chip, to).wait_send()
+                share_copy(chip, to).wait_send()
 
         half_copy().wait_send()
 
@@ -121,15 +141,6 @@
     per_piece = chunks // PIECES
     stat_rows = per_piece * groups
 
-    loads = [
-        pltpu.make_async_copy(src, dst, in_sem.at[i])
-        for i, (src, dst) in enumerate(
-            ((k_hbm, k), (v_hbm, v), (q_hbm, q), (g_hbm, g), (gain_hbm, gain_ref))
-        )
-    ]
-    for load in loads:
-        load.start()
-
     barrier = pltpu.get_barrier_semaphore()
     pl.semaphore_signal(
         barrier, inc=1, device_id={"seq": chip * 2 + (1 - core)}, device_id_type=MESH
@@ -144,6 +155,15 @@
             barrier, inc=1, device_id={"head": lax.rem(head_index + step, heads)},
             device_id_type=MESH,
         )
+
+    loads = [
+        pltpu.make_async_copy(src, dst, in_sem.at[i])
+        for i, (src, dst) in enumerate(
+            ((k_hbm, k), (v_hbm, v), (q_hbm, q), (g_hbm, g), (gain_hbm, gain_ref))
+        )
+    ]
+    for load in loads:
+        load.start()
 
     def rows(c):
         return pl.ds(pl.multiple_of(c * CHUNK, CHUNK), CHUNK)
@@ -346,14 +366,15 @@
     stat_rows = 2 * tokens // HEAD_DIM // PIECES
     wide = (tokens, width)
     square = (HEAD_DIM, HEAD_DIM)
-    half = (HEAD_DIM // 2, HEAD_DIM)
+    share = (SHARE, HEAD_DIM)
+    swapped = (HEAD_DIM - SHARE, HEAD_DIM)
     link = [
         pltpu.VMEM(square, F32),
         pltpu.VMEM(square, F32),
-        pltpu.VMEM(half, F32),
-        pltpu.VMEM((chips,) + half, F32),
-        pltpu.VMEM(half, F32),
-        pltpu.VMEM(half, F32),
+        pltpu.VMEM(share, F32),
+        pltpu.VMEM((chips,) + swapped, F32),
+        pltpu.VMEM(swapped, F32),
+        pltpu.VMEM(swapped, F32),
         pltpu.VMEM(square, F32),
     ]
     hbm = pl.BlockSpec(memory_space=pltpu.HBM)
@@ -390,7 +411,7 @@
         + link
         + [
             dma((5,)), dma((PIECES, heads)), dma((PIECES, heads)),
-            dma((2,)), dma((2,)), dma((2, chips)), dma((2, chips)), dma((2,)), dma((2,)),
+            dma((2,)), dma((2,)), dma((2, chips, 2)), dma((2, chips, 2)), dma((2,)), dma((2,)),
         ],
         compiler_params=pltpu.CompilerParams(
             collective_id=0, has_side_effects=True, vmem_limit_bytes=32 * 1024 * 1024

time: 24.7 us -> 24.1 us (0.976)
  Pallas kernels: 23.9 us -> 23.3 us
    pallas_call x1, Pallas kernels: 22.5 us -> 21.9 us  [body(): pl.pallas_call(functools.partial(kernel, chips, heads, width * heads), ou...]
where the time goes in v4:
time: 24.1 us; the launch traced here: 23.9 us
  Pallas kernels  23.3 us (97%)
  between operations  0.64 us (3%)
    pallas_call x1, Pallas kernels, body(): pl.pallas_call(functools.partial(kernel, chips, heads, width * heads), ou...  21.9 us
    pallas_call x1, Pallas kernels, body(): pl.pallas_call(last_kernel, out_shape=[jax.ShapeDtypeStruct(wide, BF16)]...  1.39 us

profile of v4, /device:TPU:0, one launch (start us, length us, event | category | flops | bytes accessed | tf_op | source)
XLA Modules:
  0.0 23.9 jit_solution(2584528240672769247)
XLA Ops:
  0.6 21.9 %shard_map.84 = (bf16[2048,128]{1,0:T(8,128)(2,1)S(1)}, bf16[2048,128]{1,0:T(8,128)(2,1)S(1)}, f32[2048,128]{1,0:T(8,128)S(1)}, f32[2048,128]{1,0:T(8,128)S(1)},...) custom-call(bf16[2048,128]{1,0:T(8,128)(2,1)} %q_hbm.1, ...), custom_call_target="tpu_custom_call" | custom-call | tf_op jit(solution)/shard_map/pallas_call | solution.py:383
  22.6 1.4 %shard_map.85 = (bf16[2048,128]{1,0:T(8,128)(2,1)}, bf16[2048,128]{1,0:T(8,128)(2,1)}, bf16[2048,128]{1,0:T(8,128)(2,1)}, bf16[2048,128]{1,0:T(8,128)(2,1)}) custom-call(bf16[2048,128]{1,0:T(8,128)(2,1)S(1)} %get-tuple-element.11.normed, bf16[2048,128]{1,0:T(8,128)(2,1)S(1)} %get-tuple-element.12.qg, f32[2048,128]{1,0:T(8,128)S(1)} %get-tuple-element.13.kpart, ...), custom_call_target="tpu_custom_call" | custom-call | tf_op jit(solution)/shard_map/pallas_call | solution.py:423
